TPU v7x, 32 devices: a whole 2x2x4 slice. The times are simulated.
32 devices in a mesh: wide: 8 (over z, core), narrow: 4 (over y, x).
Axes of the slice: x: 2, y: 2, z: 4, core: 2. Of those that a mesh axis runs over, the one named last changes fastest.
Arguments:
- query_left: float32 [288, 4, 8, 5120], P('wide', 'narrow'), may hold values from -0.078125 to 0.078125
- query_right: float32 [288, 8, 13824], P('wide', None, 'narrow'), may hold values from -0.0017089844 to 0.0017089844
- acts: bfloat16 [8, 128, 5120], P('wide'), may hold values from -6 to 6
- grads: bfloat16 [8, 128, 13824], P('wide', None, 'narrow'), may hold values from -6 to 6
- order: int32 [8], replicated, may hold values from 0 to 7, each once
Outputs:
- scores: float32 [288, 8], P('wide')
Inputs may be any that keep to these rules, and one draw needn't show every extreme that they name: order names every training example exactly once.
All inputs are finite; a program needn't handle non-finite values.
Results may differ from a plain program's by a relative error of at most 0.0003.
Values may be sent and summed in bfloat16 or wider, within the bound.
A program may use at most 64 MiB of HBM per device.

v0:
```python
import jax
import jax.numpy as jnp
from jax import lax
from jax.sharding import PartitionSpec as P


def spread(block, axis, holder):
    block = jnp.where(lax.axis_index(axis) == holder, block, jnp.zeros_like(block))
    return lax.psum(block, axis)


def block_scores(left_flat, right_flat, act_part, grad_part, queries):
    count = act_part.shape[0]
    tokens = act_part.shape[1]
    act_rows = act_part.astype(jnp.float32).reshape(count * tokens, act_part.shape[2])
    grad_rows = grad_part.astype(jnp.float32).reshape(count * tokens, grad_part.shape[2])
    dims = (((1,), (1,)), ((), ()))
    left_proj = lax.dot_general(
        left_flat,
        act_rows,
        dims,
        precision=lax.Precision.HIGHEST,
        preferred_element_type=jnp.float32,
    )
    right_proj = lax.dot_general(
        right_flat,
        grad_rows,
        dims,
        precision=lax.Precision.HIGHEST,
        preferred_element_type=jnp.float32,
    )
    product = (left_proj * right_proj).reshape(
        queries, left_flat.shape[0] // queries, count, tokens
    )
    return jnp.sum(product, axis=(1, 3))


def body(query_left, query_right, acts, grads, order):
    queries = query_left.shape[0]
    ranks = query_left.shape[2]
    left_flat = query_left.reshape(queries * ranks, query_left.shape[3])
    right_flat = query_right.reshape(queries * ranks, query_right.shape[2])
    owners = lax.axis_size("wide")
    per_owner = acts.shape[0]
    total_count = owners * per_owner
    empty = jnp.zeros((queries, total_count), jnp.float32)

    def turn_step(turn, carry):
        act_part, grad_part = (spread(acts, "wide", turn), spread(grads, "wide", turn))
        part = block_scores(left_flat, right_flat, act_part, grad_part, queries)
        part = lax.psum(part, "narrow")
        return lax.dynamic_update_slice(
            carry, part, (jnp.int32(0), (turn * per_owner).astype(jnp.int32))
        )

    raw = lax.fori_loop(0, owners, turn_step, empty)
    picker = (
        lax.broadcasted_iota(jnp.int32, (total_count, total_count), 0) == order[None, :]
    ).astype(jnp.float32)
    return jnp.dot(raw, picker, precision=lax.Precision.HIGHEST, preferred_element_type=jnp.float32)


def solution(mesh):
    return jax.shard_map(
        body,
        mesh=mesh,
        in_specs=(
            P("wide", "narrow", None, None),
            P("wide", None, "narrow"),
            P("wide", None, None),
            P("wide", None, "narrow"),
            P(),
        ),
        out_specs=P("wide", None),
        check_vma=False,
    )
```

profile of v0, /device:TPU:0, one launch (start us, length us, event | category | flops | bytes accessed | tf_op | source)
XLA Modules:
  0.0 697.8 jit_solution(4232144515138118380)
XLA Ops:
  6.5 683.6 %while.13 = (s32[]{:T(128)}, f32[36,8]{0,1:T(8,128)S(1)}, bf16[1,128,5120]{2,1,0:T(8,128)(2,1)}, f32[288,5120]{1,0:T(8,128)}, bf16[1,128,3456]{2,1,0:T(8,128)(2,...) while((s32[]{:T(128)}, f32[36,8]{0,1:T(8,128)S(1)}, ...), condition=%wide.region_6.7_spmd, body=%wide.region_0.6_spmd.sunk | while | flops 3796017152 | bytes 52942324 | solution.py:56
  10.2 67.7 %all-reduce.5.cloned.1.call-done = (bf16[128,5120]{1,0:T(8,128)(2,1)}, bf16[128,3456]{1,0:T(8,128)(2,1)}) async-done(((bf16[128,5120]{1,0:T(8,128)(2,1)}, bf16[128,3456]{1,0:T(8,128)(2,1)}), (bf16[128,5120]{1,0:T(8,128)(2,1)}, bf16[128,3456]{1,0:T(8,128)(2,1)})) %all-reduce.5.cloned.1.call-update) | async-done | bytes 2195472 | tf_op jit(solution)/shard_map/while/body/eval_jaxpr/psum | solution.py:9
  77.8 6.0 fusion.19
  86.1 9.8 %psum.34 = f32[36,1]{0,1:T(1,128)S(1)} all-reduce(f32[36,1]{0,1:T(1,128)S(1)} %bitcast.28), channel_id=1, replica_groups=mesh['wide'=8,'narrow'=4] {'narrow'}, use_global_device_ids=true, to_apply=%region_5.5 | all-reduce | flops 36 | bytes 288 | tf_op jit(solution)/shard_map/while/body/eval_jaxpr/psum | solution.py:51
  98.6 64.1 %all-reduce.5.cloned.1.call-done = (bf16[128,5120]{1,0:T(8,128)(2,1)}, bf16[128,3456]{1,0:T(8,128)(2,1)}) async-done(((bf16[128,5120]{1,0:T(8,128)(2,1)}, bf16[128,3456]{1,0:T(8,128)(2,1)}), (bf16[128,5120]{1,0:T(8,128)(2,1)}, bf16[128,3456]{1,0:T(8,128)(2,1)})) %all-reduce.5.cloned.1.call-update) | async-done | bytes 2195472 | tf_op jit(solution)/shard_map/while/body/eval_jaxpr/psum | solution.py:9
  162.7 6.0 fusion.19
  171.0 9.8 %psum.34 = f32[36,1]{0,1:T(1,128)S(1)} all-reduce(f32[36,1]{0,1:T(1,128)S(1)} %bitcast.28), channel_id=1, replica_groups=mesh['wide'=8,'narrow'=4] {'narrow'}, use_global_device_ids=true, to_apply=%region_5.5 | all-reduce | flops 36 | bytes 288 | tf_op jit(solution)/shard_map/while/body/eval_jaxpr/psum | solution.py:51
  183.5 64.2 %all-reduce.5.cloned.1.call-done = (bf16[128,5120]{1,0:T(8,128)(2,1)}, bf16[128,3456]{1,0:T(8,128)(2,1)}) async-done(((bf16[128,5120]{1,0:T(8,128)(2,1)}, bf16[128,3456]{1,0:T(8,128)(2,1)}), (bf16[128,5120]{1,0:T(8,128)(2,1)}, bf16[128,3456]{1,0:T(8,128)(2,1)})) %all-reduce.5.cloned.1.call-update) | async-done | bytes 2195472 | tf_op jit(solution)/shard_map/while/body/eval_jaxpr/psum | solution.py:9
  247.6 6.0 fusion.19
  255.9 9.8 %psum.34 = f32[36,1]{0,1:T(1,128)S(1)} all-reduce(f32[36,1]{0,1:T(1,128)S(1)} %bitcast.28), channel_id=1, replica_groups=mesh['wide'=8,'narrow'=4] {'narrow'}, use_global_device_ids=true, to_apply=%region_5.5 | all-reduce | flops 36 | bytes 288 | tf_op jit(solution)/shard_map/while/body/eval_jaxpr/psum | solution.py:51
  268.4 63.8 %all-reduce.5.cloned.1.call-done = (bf16[128,5120]{1,0:T(8,128)(2,1)}, bf16[128,3456]{1,0:T(8,128)(2,1)}) async-done(((bf16[128,5120]{1,0:T(8,128)(2,1)}, bf16[128,3456]{1,0:T(8,128)(2,1)}), (bf16[128,5120]{1,0:T(8,128)(2,1)}, bf16[128,3456]{1,0:T(8,128)(2,1)})) %all-reduce.5.cloned.1.call-update) | async-done | bytes 2195472 | tf_op jit(solution)/shard_map/while/body/eval_jaxpr/psum | solution.py:9
  332.2 6.0 fusion.19
  340.5 9.8 %psum.34 = f32[36,1]{0,1:T(1,128)S(1)} all-reduce(f32[36,1]{0,1:T(1,128)S(1)} %bitcast.28), channel_id=1, replica_groups=mesh['wide'=8,'narrow'=4] {'narrow'}, use_global_device_ids=true, to_apply=%region_5.5 | all-reduce | flops 36 | bytes 288 | tf_op jit(solution)/shard_map/while/body/eval_jaxpr/psum | solution.py:51
  353.0 64.1 %all-reduce.5.cloned.1.call-done = (bf16[128,5120]{1,0:T(8,128)(2,1)}, bf16[128,3456]{1,0:T(8,128)(2,1)}) async-done(((bf16[128,5120]{1,0:T(8,128)(2,1)}, bf16[128,3456]{1,0:T(8,128)(2,1)}), (bf16[128,5120]{1,0:T(8,128)(2,1)}, bf16[128,3456]{1,0:T(8,128)(2,1)})) %all-reduce.5.cloned.1.call-update) | async-done | bytes 2195472 | tf_op jit(solution)/shard_map/while/body/eval_jaxpr/psum | solution.py:9
  425.4 9.8 %psum.34 = f32[36,1]{0,1:T(1,128)S(1)} all-reduce(f32[36,1]{0,1:T(1,128)S(1)} %bitcast.28), channel_id=1, replica_groups=mesh['wide'=8,'narrow'=4] {'narrow'}, use_global_device_ids=true, to_apply=%region_5.5 | all-reduce | flops 36 | bytes 288 | tf_op jit(solution)/shard_map/while/body/eval_jaxpr/psum | solution.py:51
  437.9 63.7 %all-reduce.5.cloned.1.call-done = (bf16[128,5120]{1,0:T(8,128)(2,1)}, bf16[128,3456]{1,0:T(8,128)(2,1)}) async-done(((bf16[128,5120]{1,0:T(8,128)(2,1)}, bf16[128,3456]{1,0:T(8,128)(2,1)}), (bf16[128,5120]{1,0:T(8,128)(2,1)}, bf16[128,3456]{1,0:T(8,128)(2,1)})) %all-reduce.5.cloned.1.call-update) | async-done | bytes 2195472 | tf_op jit(solution)/shard_map/while/body/eval_jaxpr/psum | solution.py:9
  501.6 6.0 fusion.19
  509.9 9.8 %psum.34 = f32[36,1]{0,1:T(1,128)S(1)} all-reduce(f32[36,1]{0,1:T(1,128)S(1)} %bitcast.28), channel_id=1, replica_groups=mesh['wide'=8,'narrow'=4] {'narrow'}, use_global_device_ids=true, to_apply=%region_5.5 | all-reduce | flops 36 | bytes 288 | tf_op jit(solution)/shard_map/while/body/eval_jaxpr/psum | solution.py:51
  522.4 64.7 %all-reduce.5.cloned.1.call-done = (bf16[128,5120]{1,0:T(8,128)(2,1)}, bf16[128,3456]{1,0:T(8,128)(2,1)}) async-done(((bf16[128,5120]{1,0:T(8,128)(2,1)}, bf16[128,3456]{1,0:T(8,128)(2,1)}), (bf16[128,5120]{1,0:T(8,128)(2,1)}, bf16[128,3456]{1,0:T(8,128)(2,1)})) %all-reduce.5.cloned.1.call-update) | async-done | bytes 2195472 | tf_op jit(solution)/shard_map/while/body/eval_jaxpr/psum | solution.py:9
  587.1 6.0 fusion.19
  595.4 9.8 %psum.34 = f32[36,1]{0,1:T(1,128)S(1)} all-reduce(f32[36,1]{0,1:T(1,128)S(1)} %bitcast.28), channel_id=1, replica_groups=mesh['wide'=8,'narrow'=4] {'narrow'}, use_global_device_ids=true, to_apply=%region_5.5 | all-reduce | flops 36 | bytes 288 | tf_op jit(solution)/shard_map/while/body/eval_jaxpr/psum | solution.py:51
  607.9 64.1 %all-reduce.5.cloned.1.call-done = (bf16[128,5120]{1,0:T(8,128)(2,1)}, bf16[128,3456]{1,0:T(8,128)(2,1)}) async-done(((bf16[128,5120]{1,0:T(8,128)(2,1)}, bf16[128,3456]{1,0:T(8,128)(2,1)}), (bf16[128,5120]{1,0:T(8,128)(2,1)}, bf16[128,3456]{1,0:T(8,128)(2,1)})) %all-reduce.5.cloned.1.call-update) | async-done | bytes 2195472 | tf_op jit(solution)/shard_map/while/body/eval_jaxpr/psum | solution.py:9
  672.0 6.0 fusion.19
  680.3 9.9 %psum.34 = f32[36,1]{0,1:T(1,128)S(1)} all-reduce(f32[36,1]{0,1:T(1,128)S(1)} %bitcast.28), channel_id=1, replica_groups=mesh['wide'=8,'narrow'=4] {'narrow'}, use_global_device_ids=true, to_apply=%region_5.5 | all-reduce | flops 36 | bytes 288 | tf_op jit(solution)/shard_map/while/body/eval_jaxpr/psum | solution.py:51
  (117 shorter events, 46.8 us)
Async XLA Ops:
  6.5 683.6 %copy-start.3 = (s32[8]{0:T(128)S(1)}, s32[8]{0:T(128)}, u32[]{:S(2)}) copy-start(s32[8]{0:T(128)} %param.11) | copy-start | bytes 100
  6.5 71.3 %all-reduce.5.cloned.1.call-start = ((), (), s32[]{:S(2)}) async-start(), calls=%async_computation | async-start | bytes 4390912 | tf_op jit(solution)/shard_map/while/body/eval_jaxpr/psum | solution.py:9
  77.8 6.0 copy-start
  77.8 6.0 copy-start.2
  96.0 66.7 %all-reduce.5.cloned.1.call-start = ((), (), s32[]{:S(2)}) async-start(), calls=%async_computation | async-start | bytes 4390912 | tf_op jit(solution)/shard_map/while/body/eval_jaxpr/psum | solution.py:9
  162.7 6.0 copy-start
  162.7 6.0 copy-start.2
  180.8 66.8 %all-reduce.5.cloned.1.call-start = ((), (), s32[]{:S(2)}) async-start(), calls=%async_computation | async-start | bytes 4390912 | tf_op jit(solution)/shard_map/while/body/eval_jaxpr/psum | solution.py:9
  247.6 6.0 copy-start
  247.6 6.0 copy-start.2
  265.8 66.4 %all-reduce.5.cloned.1.call-start = ((), (), s32[]{:S(2)}) async-start(), calls=%async_computation | async-start | bytes 4390912 | tf_op jit(solution)/shard_map/while/body/eval_jaxpr/psum | solution.py:9
  332.2 6.0 copy-start
  332.2 6.0 copy-start.2
  350.4 66.7 %all-reduce.5.cloned.1.call-start = ((), (), s32[]{:S(2)}) async-start(), calls=%async_computation | async-start | bytes 4390912 | tf_op jit(solution)/shard_map/while/body/eval_jaxpr/psum | solution.py:9
  417.1 6.0 copy-start.2
  435.3 66.4 %all-reduce.5.cloned.1.call-start = ((), (), s32[]{:S(2)}) async-start(), calls=%async_computation | async-start | bytes 4390912 | tf_op jit(solution)/shard_map/while/body/eval_jaxpr/psum | solution.py:9
  501.6 6.0 copy-start
  501.6 6.0 copy-start.2
  519.8 67.3 %all-reduce.5.cloned.1.call-start = ((), (), s32[]{:S(2)}) async-start(), calls=%async_computation | async-start | bytes 4390912 | tf_op jit(solution)/shard_map/while/body/eval_jaxpr/psum | solution.py:9
  587.1 6.0 copy-start
  587.1 6.0 copy-start.2
  605.2 66.7 %all-reduce.5.cloned.1.call-start = ((), (), s32[]{:S(2)}) async-start(), calls=%async_computation | async-start | bytes 4390912 | tf_op jit(solution)/shard_map/while/body/eval_jaxpr/psum | solution.py:9
  672.0 6.0 copy-start
  672.0 6.0 copy-start.2
  (9 other events, 19.2 us)
Sparse Core Ops, SparseCore 0:
  10.3 67.5 all-reduce.4
  99.3 63.3 all-reduce.4
  184.1 63.4 all-reduce.4
  268.8 63.4 all-reduce.4
  353.4 63.7 all-reduce.4
  438.2 63.3 all-reduce.4
  523.1 63.9 all-reduce.4
  608.5 63.3 all-reduce.4
where the time goes:
time: 698 us
  waiting for transfers between devices  517 us (74%)
  blocking collectives  78.8 us (11%)
  matrix products  65 us (9%)
  other arithmetic  19.9 us (3%)
  between operations  13.4 us (2%)
    psum x8, waiting for transfers between devices, spread(): return lax.psum(block, axis)  516 us
    psum x8, blocking collectives, turn_step(): part = lax.psum(part, 'narrow')  78.8 us
    dot_general x8, matrix products, block_scores(): lax.dot_general(left_flat, act_rows, dims, precision=lax.Precision.HIGHES...  47.8 us
    dot_general x8, matrix products, block_scores(): lax.dot_general(right_flat, grad_rows, dims, precision=lax.Precision.HIGH...  16.4 us
  transfers between devices with their start and end apart: 8, of which 8 were waited for; matrix products, arithmetic and copies ran while one was open for 0% of the time, Pallas kernels for 0%

commit v1 on v0

v1 whole, which is shorter than its diff:
```python
import functools

import jax
import jax.numpy as jnp
from jax import lax
from jax.experimental import pallas as pl
from jax.experimental.pallas import tpu as pltpu
from jax.sharding import PartitionSpec as P

CORES = 2
CHUNKS = 4
MESH = pl.DeviceIdType.MESH


def kernel(
    levels, narrow, left_hbm, right_hbm, acts_hbm, grads_hbm, raw_out,
    acts_all, grads_all, left_in, right_in, left_two, right_two, x_ref, total, parts,
    load_sem, za_send, za_recv, zg_send, zg_recv, pa_send, pa_recv,
    ca_send, ca_recv, cg_send, cg_recv, sum_send, sum_recv,
):
    wide_at = lax.axis_index("wide")
    me = lax.axis_index("narrow")
    z = lax.div(wide_at, CORES)
    core = lax.rem(wide_at, CORES)
    other = z * CORES + (1 - core)
    tokens, width = acts_hbm.shape[1:]
    rows = left_hbm.shape[0]
    queries = raw_out.shape[0]
    ranks = rows // queries

    row_parts = min(narrow, tokens // 16)
    col_parts = narrow // row_parts
    piece_rows, piece_cols = tokens // row_parts, width // col_parts
    chunk_rows = tokens // CHUNKS

    def piece(n):
        row = pl.multiple_of(lax.rem(n, row_parts) * piece_rows, piece_rows)
        if col_parts == 1:
            return (pl.ds(row, piece_rows), slice(None))
        col = pl.multiple_of(lax.div(n, row_parts) * piece_cols, piece_cols)
        return (pl.ds(row, piece_rows), pl.ds(col, piece_cols))

    def acts_at(example, n):
        return acts_all.at[(example, *piece(n))]

    def grads_at(example, g):
        return grads_all.at[example, pl.ds(g * chunk_rows, chunk_rows), :]

    def send(src, dst, send_sem, recv_sem, **where):
        return pltpu.make_async_remote_copy(
            src_ref=src, dst_ref=dst, send_sem=send_sem, recv_sem=recv_sem,
            device_id=where, device_id_type=MESH,
        )

    def z_acts(level, way, target, src=None):
        slot = acts_at(level * CORES + core, me)
        return send(slot if src is None else src, slot, za_send.at[level, way], za_recv.at[level], wide=target)

    def z_grads(level, way, target, g, src=None):
        slot = grads_at(level * CORES + core, g)
        return send(slot if src is None else src, slot, zg_send.at[level, way, g], zg_recv.at[level, g], wide=target)

    def plane_acts(level, n, target):
        slot = acts_at(level * CORES + core, n)
        return send(slot, slot, pa_send.at[level, target], pa_recv.at[level, n], narrow=target)

    def core_acts(level, n, whose, src=None):
        slot = acts_at(level * CORES + whose, n)
        return send(slot if src is None else src, slot, ca_send.at[level, n], ca_recv.at[level, n], wide=other)

    def core_grads(level, g, whose, src=None):
        slot = grads_at(level * CORES + whose, g)
        return send(slot if src is None else src, slot, cg_send.at[level, g], cg_recv.at[level, g], wide=other)

    barrier = pltpu.get_barrier_semaphore()
    up, down = z + 1 < levels, z > 0

    @pl.when(up)
    def _():
        pl.semaphore_signal(barrier, inc=1, device_id={"wide": wide_at + CORES}, device_id_type=MESH)

    @pl.when(down)
    def _():
        pl.semaphore_signal(barrier, inc=1, device_id={"wide": wide_at - CORES}, device_id_type=MESH)

    pl.semaphore_signal(barrier, inc=1, device_id={"wide": other}, device_id_type=MESH)
    for j in range(1, narrow):
        pl.semaphore_signal(barrier, inc=1, device_id={"narrow": lax.rem(me + j, narrow)}, device_id_type=MESH)
    pl.semaphore_wait(barrier, narrow + up.astype(jnp.int32) + down.astype(jnp.int32))

    own_acts = acts_hbm.at[(0, *piece(me))]

    def own_grads(g):
        return grads_hbm.at[0, pl.ds(g * chunk_rows, chunk_rows), :]

    for way, ok in ((0, up), (1, down)):
        target = wide_at + (CORES if way == 0 else -CORES)

        @pl.when(ok)
        def _():
            z_acts(z, way, target, own_acts).start()
            for g in range(CHUNKS):
                z_grads(z, way, target, g, own_grads(g)).start()

    for n in range(narrow):
        core_acts(z, n, core, acts_hbm.at[(0, *piece(n))]).start()
    for g in range(CHUNKS):
        core_grads(z, g, core, own_grads(g)).start()

    loads = [
        pltpu.make_async_copy(left_hbm, left_in, load_sem.at[0]),
        pltpu.make_async_copy(right_hbm, right_in, load_sem.at[1]),
        pltpu.make_async_copy(acts_hbm.at[0], acts_all.at[wide_at], load_sem.at[2]),
        pltpu.make_async_copy(grads_hbm.at[0], grads_all.at[wide_at], load_sem.at[3]),
    ]
    for load in loads:
        load.start()
    total[...] = jnp.zeros_like(total)

    def split(src, dst):
        def step(i, carry):
            row = pl.multiple_of(i * 32, 32)
            value = src[pl.ds(row, 32), :]
            high = value.astype(jnp.bfloat16)
            dst[pl.ds(row, 32), :] = high
            dst[pl.ds(rows + row, 32), :] = (value - high.astype(jnp.float32)).astype(jnp.bfloat16)
            return carry

        lax.fori_loop(0, rows // 32, step, 0)

    loads[0].wait()
    split(left_in, left_two)
    loads[1].wait()
    split(right_in, right_two)
    loads[2].wait()
    loads[3].wait()

    def project(two, ref, level):
        block = ref[pl.ds(level * CORES, CORES)]
        block = block.reshape(CORES * tokens, block.shape[2])
        both = lax.dot_general(two[...], block, (((1,), (1,)), ((), ())), preferred_element_type=jnp.float32)
        return both[:rows] + both[rows:]

    def work(level):
        for n in range(narrow):
            core_acts(level, n, 1 - core).wait_recv()
        x_ref[...] = project(left_two, acts_all, level)
        for g in range(CHUNKS):
            core_grads(level, g, 1 - core).wait_recv()
        product = x_ref[...] * project(right_two, grads_all, level)
        by_query = jnp.sum(product.reshape(queries, ranks, CORES * tokens), axis=1)
        column = lax.broadcasted_iota(jnp.int32, total.shape, 1)
        for c in range(CORES):
            score = jnp.sum(by_query[:, c * tokens:(c + 1) * tokens], axis=1, keepdims=True)
            total[...] += jnp.where(column == level * CORES + c, score, 0.0)

    def step(i, carry):
        way = lax.rem(i, 2)
        sign = 1 - 2 * way
        level = z - sign * (lax.div(i, 2) + 1)
        following = z + sign

        @pl.when(jnp.logical_and(level >= 0, level < levels))
        def _():
            onward = jnp.logical_and(following >= 0, following < levels)
            target = following * CORES + core
            z_acts(level, way, wide_at).wait_recv()

            @pl.when(onward)
            def _():
                z_acts(level, way, target).start()

            for j in range(1, narrow):
                plane_acts(level, me, lax.rem(me + j, narrow)).start()
            core_acts(level, me, core).start()
            for g in range(CHUNKS):
                z_grads(level, way, wide_at, g).wait_recv()

                @pl.when(onward)
                def _():
                    z_grads(level, way, target, g).start()

                core_grads(level, g, core).start()
            for j in range(1, narrow):
                n = lax.rem(me + j, narrow)
                plane_acts(level, n, me).wait_recv()
                core_acts(level, n, core).start()
            work(level)

        return carry

    work(z)
    lax.fori_loop(0, 2 * (levels - 1), step, 0)

    parts[me] = total[...]

    def sums(target, n):
        return send(total, parts.at[n], sum_send.at[target], sum_recv.at[n], narrow=target)

    for j in range(1, narrow):
        sums(lax.rem(me + j, narrow), me).start()

    for n in range(narrow):
        core_acts(z, n, core).wait_send()
    for g in range(CHUNKS):
        core_grads(z, g, core).wait_send()
    for way, ok in ((0, up), (1, down)):
        target = wide_at + (CORES if way == 0 else -CORES)

        @pl.when(ok)
        def _():
            z_acts(z, way, target).wait_send()
            for g in range(CHUNKS):
                z_grads(z, way, target, g).wait_send()

    def drain(i, carry):
        way = lax.rem(i, 2)
        sign = 1 - 2 * way
        level = z - sign * (lax.div(i, 2) + 1)
        following = z + sign

        @pl.when(jnp.logical_and(level >= 0, level < levels))
        def _():
            @pl.when(jnp.logical_and(following >= 0, following < levels))
            def _():
                target = following * CORES + core
                z_acts(level, way, target).wait_send()
                for g in range(CHUNKS):
                    z_grads(level, way, target, g).wait_send()

            for j in range(1, narrow):
                plane_acts(level, me, lax.rem(me + j, narrow)).wait_send()
            for n in range(narrow):
                core_acts(level, n, core).wait_send()
            for g in range(CHUNKS):
                core_grads(level, g, core).wait_send()

        return carry

    lax.fori_loop(0, 2 * (levels - 1), drain, 0)
    for j in range(1, narrow):
        sums(me, lax.rem(me + j, narrow)).wait_recv()
    raw = parts[0]
    for n in range(1, narrow):
        raw += parts[n]
    raw_out[...] = raw
    for j in range(1, narrow):
        sums(lax.rem(me + j, narrow), me).wait_send()


def body(query_left, query_right, acts, grads, order):
    queries, _, ranks, width = query_left.shape
    block = query_right.shape[2]
    rows = queries * ranks
    owners, narrow = lax.axis_size("wide"), lax.axis_size("narrow")
    levels = owners // CORES
    tokens = acts.shape[1]
    dma = pltpu.SemaphoreType.DMA
    hbm = pl.BlockSpec(memory_space=pl.ANY)
    raw = pl.pallas_call(
        functools.partial(kernel, levels, narrow),
        out_shape=jax.ShapeDtypeStruct((queries, 128), jnp.float32),
        in_specs=[hbm] * 4,
        out_specs=pl.BlockSpec(memory_space=pltpu.VMEM),
        scratch_shapes=[
            pltpu.VMEM((owners, tokens, width), jnp.bfloat16),
            pltpu.VMEM((owners, tokens, block), jnp.bfloat16),
            pltpu.VMEM((rows, width), jnp.float32),
            pltpu.VMEM((rows, block), jnp.float32),
            pltpu.VMEM((2 * rows, width), jnp.bfloat16),
            pltpu.VMEM((2 * rows, block), jnp.bfloat16),
            pltpu.VMEM((rows, CORES * tokens), jnp.float32),
            pltpu.VMEM((queries, 128), jnp.float32),
            pltpu.VMEM((narrow, queries, 128), jnp.float32),
            dma((4,)),
            dma((levels, 2)), dma((levels,)),
            dma((levels, 2, CHUNKS)), dma((levels, CHUNKS)),
            dma((levels, narrow)), dma((levels, narrow)),
            dma((levels, narrow)), dma((levels, narrow)),
            dma((levels, CHUNKS)), dma((levels, CHUNKS)),
            dma((narrow,)), dma((narrow,)),
        ],
        compiler_params=pltpu.CompilerParams(
            collective_id=0, has_side_effects=True, vmem_limit_bytes=58 * 1024 * 1024,
        ),
        cost_estimate=pl.CostEstimate(
            flops=4 * rows * owners * tokens * (width + block),
            bytes_accessed=4 * rows * (width + block), transcendentals=0,
        ),
        name="scores",
    )(
        query_left.reshape(rows, width),
        query_right.reshape(rows, block),
        acts,
        grads,
    )
    picker = (lax.broadcasted_iota(jnp.int32, (owners, owners), 0) == order[None, :]).astype(jnp.float32)
    return jnp.sum(raw[:, :owners, None] * picker[None], axis=1)


def solution(mesh):
    return jax.shard_map(
        body,
        mesh=mesh,
        in_specs=(
            P("wide", "narrow", None, None),
            P("wide", None, "narrow"),
            P("wide", None, None),
            P("wide", None, "narrow"),
            P(),
        ),
        out_specs=P("wide", None),
        check_vma=False,
    )
```

time: 698 us -> 107 us (0.15)
  waiting for transfers between devices: 517 us -> 0 us
  Pallas kernels: 0 us -> 105 us
  blocking collectives: 78.8 us -> 0 us
  matrix products: 65 us -> 0 us
  other arithmetic: 19.9 us -> 0.68 us
  between operations: 13.4 us -> 0.01 us
    psum x8 -> x0, waiting for transfers between devices: 516 us -> none  [spread(): return lax.psum(block, axis)]
    pallas_call x0 -> x1, Pallas kernels: none -> 105 us  [body(): pl.pallas_call(functools.partial(kernel, levels, narrow), out_shape=jax.S...]
    psum x8 -> x0, blocking collectives: 78.8 us -> none  [turn_step(): part = lax.psum(part, 'narrow')]
    dot_general x17 -> x0, matrix products: 65 us -> none  [the longest x8 47.8 us: block_scores(): lax.dot_general(left_flat, act_rows, dims, precision=lax.Precision.HIGHES...]
    reshape x16 -> x0, other arithmetic: 19 us -> none  [the longest x8 10.8 us: block_scores(): act_part.astype(jnp.float32).reshape(count * tokens, act_part.shape[2])]
  transfers between devices with their start and end apart: 8 -> 0, of which waited for: 8 -> 0; matrix products, arithmetic and copies ran while one was open for 0% -> 0% of each run, Pallas kernels for 0% -> 0%
where the time goes in v1:
time: 107 us
  Pallas kernels  105 us (98%)
    pallas_call x1, Pallas kernels, body(): pl.pallas_call(functools.partial(kernel, levels, narrow), out_shape=jax.S...  105 us

profile of v1, /device:TPU:0, one launch (start us, length us, event | category | flops | bytes accessed | tf_op | source)
XLA Modules:
  0.0 106.8 jit_solution(2940416537666631841)
XLA Ops:
  0.0 0.0 copy-start
  0.0 105.3 %scores.1 = f32[36,128]{1,0:T(8,128)} custom-call(f32[288,5120]{1,0:T(8,128)} %bitcast.4, f32[288,3456]{1,0:T(8,128)} %bitcast.5, bf16[1,128,5120]{2,1,0:T(8,128)(2,1)} %acts_hbm.1, bf16[1,128,3456]{2,1,0:T(8,128)(2,1)} %grads_hbm.1), custom_call_target="tpu_custom_call" | custom-call | flops 10116661248 | bytes 9879552 | tf_op jit(solution)/shard_map/scores/pallas_call | solution.py:260
  105.3 0.8 copy.6
  106.1 0.0 copy-done
  106.1 0.7 multiply_reduce_fusion
  (1 shorter events, 0.0 us)
Async XLA Ops:
  0.0 106.1 %copy-start = (s32[8]{0:T(128)S(1)}, s32[8]{0:T(128)}, u32[]{:S(2)}) copy-start(s32[8]{0:T(128)} %param.9) | copy-start | bytes 100

commit v2 on v1

--- a/solution.py
+++ b/solution.py
@@ -141,56 +141,93 @@
         both = lax.dot_general(two[...], block, (((1,), (1,)), ((), ())), preferred_element_type=jnp.float32)
         return both[:rows] + both[rows:]
 
-    def work(level):
+    def left_work(level, way):
         for n in range(narrow):
             core_acts(level, n, 1 - core).wait_recv()
-        x_ref[...] = project(left_two, acts_all, level)
+        x_ref[way] = project(left_two, acts_all, level)
+
+    def right_work(level, way):
         for g in range(CHUNKS):
             core_grads(level, g, 1 - core).wait_recv()
-        product = x_ref[...] * project(right_two, grads_all, level)
+        product = x_ref[way] * project(right_two, grads_all, level)
         by_query = jnp.sum(product.reshape(queries, ranks, CORES * tokens), axis=1)
         column = lax.broadcasted_iota(jnp.int32, total.shape, 1)
         for c in range(CORES):
             score = jnp.sum(by_query[:, c * tokens:(c + 1) * tokens], axis=1, keepdims=True)
             total[...] += jnp.where(column == level * CORES + c, score, 0.0)
 
+    def arrivals(d):
+        found = []
+        for way, sign in ((0, 1), (1, -1)):
+            level, following = z - sign * d, z + sign
+            valid = jnp.logical_and(level >= 0, level < levels)
+            onward = jnp.logical_and(following >= 0, following < levels)
+            found.append((way, level, valid, jnp.logical_and(valid, onward), following * CORES + core))
+        return found
+
+    def take_grads(now, g):
+        for way, level, valid, onward, target in now:
+            @pl.when(valid)
+            def _():
+                z_grads(level, way, wide_at, g).wait_recv()
+
+            @pl.when(onward)
+            def _():
+                z_grads(level, way, target, g).start()
+
+            @pl.when(valid)
+            def _():
+                core_grads(level, g, core).start()
+
     def step(i, carry):
-        way = lax.rem(i, 2)
-        sign = 1 - 2 * way
-        level = z - sign * (lax.div(i, 2) + 1)
-        following = z + sign
-
-        @pl.when(jnp.logical_and(level >= 0, level < levels))
+        now, before = arrivals(i + 1), arrivals(i)
+        for way, level, valid, onward, target in now:
+            @pl.when(valid)
+            def _():
+                z_acts(level, way, wide_at).wait_recv()
+
+            @pl.when(onward)
+            def _():
+                z_acts(level, way, target).start()
+
+            @pl.when(valid)
+            def _():
+                for j in range(1, narrow):
+                    plane_acts(level, me, lax.rem(me + j, narrow)).start()
+                core_acts(level, me, core).start()
+
+        take_grads(now, 0)
+        for way, level, valid, _, _ in before:
+            @pl.when(jnp.logical_and(valid, i > 0))
+            def _():
+                right_work(level, way)
+
+        take_grads(now, 1)
+        for way, level, valid, _, _ in now:
+            @pl.when(valid)
+            def _():
+                for j in range(1, narrow):
+                    n = lax.rem(me + j, narrow)
+                    plane_acts(level, n, me).wait_recv()
+                    core_acts(level, n, core).start()
+
+        take_grads(now, 2)
+        for way, level, valid, _, _ in now:
+            @pl.when(valid)
+            def _():
+                left_work(level, way)
+
+        for g in range(3, CHUNKS):
+            take_grads(now, g)
+        return carry
+
+    left_work(z, 0)
+    right_work(z, 0)
+    lax.fori_loop(0, levels - 1, step, 0)
+    for way, level, valid, _, _ in arrivals(levels - 1):
+        @pl.when(valid)
         def _():
-            onward = jnp.logical_and(following >= 0, following < levels)
-            target = following * CORES + core
-            z_acts(level, way, wide_at).wait_recv()
-
-            @pl.when(onward)
-            def _():
-                z_acts(level, way, target).start()
-
-            for j in range(1, narrow):
-                plane_acts(level, me, lax.rem(me + j, narrow)).start()
-            core_acts(level, me, core).start()
-            for g in range(CHUNKS):
-                z_grads(level, way, wide_at, g).wait_recv()
-
-                @pl.when(onward)
-                def _():
-                    z_grads(level, way, target, g).start()
-
-                core_grads(level, g, core).start()
-            for j in range(1, narrow):
-                n = lax.rem(me + j, narrow)
-                plane_acts(level, n, me).wait_recv()
-                core_acts(level, n, core).start()
-            work(level)
-
-        return carry
-
-    work(z)
-    lax.fori_loop(0, 2 * (levels - 1), step, 0)
+            right_work(level, way)
 
     parts[me] = total[...]
 
@@ -269,7 +306,7 @@
             pltpu.VMEM((rows, block), jnp.float32),
             pltpu.VMEM((2 * rows, width), jnp.bfloat16),
             pltpu.VMEM((2 * rows, block), jnp.bfloat16),
-            pltpu.VMEM((rows, CORES * tokens), jnp.float32),
+            pltpu.VMEM((2, rows, CORES * tokens), jnp.float32),
             pltpu.VMEM((queries, 128), jnp.float32),
             pltpu.VMEM((narrow, queries, 128), jnp.float32),
             dma((4,)),

time: 107 us -> 94 us (0.88)
  Pallas kernels: 105 us -> 92.4 us
    pallas_call x1, Pallas kernels: 105 us -> 92.4 us  [body(): pl.pallas_call(functools.partial(kernel, levels, narrow), out_shape=jax.S...]
where the time goes in v2:
time: 94 us; the launch traced here: 93.9 us
  Pallas kernels  92.4 us (98%)
    pallas_call x1, Pallas kernels, body(): pl.pallas_call(functools.partial(kernel, levels, narrow), out_shape=jax.S...  92.4 us

profile of v2, /device:TPU:0, one launch (start us, length us, event | category | flops | bytes accessed | tf_op | source)
XLA Modules:
  0.0 93.9 jit_solution(5862752831275234347)
XLA Ops:
  0.0 0.0 copy-start
  0.0 92.4 %scores.1 = f32[36,128]{1,0:T(8,128)} custom-call(f32[288,5120]{1,0:T(8,128)} %bitcast.4, f32[288,3456]{1,0:T(8,128)} %bitcast.5, bf16[1,128,5120]{2,1,0:T(8,128)(2,1)} %acts_hbm.1, bf16[1,128,3456]{2,1,0:T(8,128)(2,1)} %grads_hbm.1), custom_call_target="tpu_custom_call" | custom-call | flops 10116661248 | bytes 9879552 | tf_op jit(solution)/shard_map/scores/pallas_call | solution.py:297
  92.4 0.8 copy.6
  93.2 0.0 copy-done
  93.2 0.7 multiply_reduce_fusion
  (1 shorter events, 0.0 us)
Async XLA Ops:
  0.0 93.2 %copy-start = (s32[8]{0:T(128)S(1)}, s32[8]{0:T(128)}, u32[]{:S(2)}) copy-start(s32[8]{0:T(128)} %param.9) | copy-start | bytes 100

commit v3 on v2

--- a/solution.py
+++ b/solution.py
@@ -180,7 +180,7 @@
                 core_grads(level, g, core).start()
 
     def step(i, carry):
-        now, before = arrivals(i + 1), arrivals(i)
+        now = arrivals(i + 1)
         for way, level, valid, onward, target in now:
             @pl.when(valid)
             def _():
@@ -197,11 +197,6 @@
                 core_acts(level, me, core).start()
 
         take_grads(now, 0)
-        for way, level, valid, _, _ in before:
-            @pl.when(jnp.logical_and(valid, i > 0))
-            def _():
-                right_work(level, way)
-
         take_grads(now, 1)
         for way, level, valid, _, _ in now:
             @pl.when(valid)
@@ -213,12 +208,18 @@
 
         take_grads(now, 2)
         for way, level, valid, _, _ in now:
-            @pl.when(valid)
+            @pl.when(jnp.logical_and(valid, i == levels - 2))
             def _():
                 left_work(level, way)
 
         for g in range(3, CHUNKS):
             take_grads(now, g)
+        for way, level, valid, _, _ in now:
+            @pl.when(jnp.logical_and(valid, i < levels - 2))
+            def _():
+                left_work(level, way)
+                right_work(level, way)
+
         return carry
 
     left_work(z, 0)

time: 94 us -> 94 us (level)
  no operation moved by 1% of the time
where the time goes in v3:
time: 94 us; the launch traced here: 93.9 us
  Pallas kernels  92.4 us (98%)
    pallas_call x1, Pallas kernels, body(): pl.pallas_call(functools.partial(kernel, levels, narrow), out_shape=jax.S...  92.4 us

profile of v3, /device:TPU:0, one launch (start us, length us, event | category | flops | bytes accessed | tf_op | source)
XLA Modules:
  0.0 93.9 jit_solution(2256896805340058976)
XLA Ops:
  0.0 0.0 copy-start
  0.0 92.4 %scores.1 = f32[36,128]{1,0:T(8,128)} custom-call(f32[288,5120]{1,0:T(8,128)} %bitcast.4, f32[288,3456]{1,0:T(8,128)} %bitcast.5, bf16[1,128,5120]{2,1,0:T(8,128)(2,1)} %acts_hbm.1, bf16[1,128,3456]{2,1,0:T(8,128)(2,1)} %grads_hbm.1), custom_call_target="tpu_custom_call" | custom-call | flops 10116661248 | bytes 9879552 | tf_op jit(solution)/shard_map/scores/pallas_call | solution.py:298
  92.4 0.8 copy.6
  93.2 0.0 copy-done
  93.2 0.7 multiply_reduce_fusion
  (1 shorter events, 0.0 us)
Async XLA Ops:
  0.0 93.2 %copy-start = (s32[8]{0:T(128)S(1)}, s32[8]{0:T(128)}, u32[]{:S(2)}) copy-start(s32[8]{0:T(128)} %param.9) | copy-start | bytes 100
